TPU v7x, 32 devices: a whole 2x2x4 slice. The times are simulated.
32 devices in a mesh: rep: 2 (over x), dp: 4 (over y, core), ctx: 4 (over z).
Axes of the slice: x: 2, y: 2, z: 4, core: 2. Of those that a mesh axis runs over, the one named last changes fastest.
Arguments:
- frames: bfloat16 [8, 512, 1024], P(('rep', 'dp'), 'ctx'), may hold values from -24 to 24
- lengths: int32 [8], P(('rep', 'dp')), may hold values from 64 to 512, as said below
- cotangent: bfloat16 [8, 512, 1024], P(('rep', 'dp'), 'ctx'), may hold values from -6 to 6
- w_query: bfloat16 [1024, 512], P('dp'), may hold values from -0.5 to 0.5
- w_key: bfloat16 [1024, 512], P('dp'), may hold values from -0.5 to 0.5
- w_value: bfloat16 [1024, 512], P('dp'), may hold values from -0.1875 to 0.1875
- w_out: bfloat16 [512, 1024], P('dp'), may hold values from -0.25 to 0.25
Outputs:
- attended: bfloat16 [8, 512, 1024], P(('rep', 'dp'), 'ctx')
- grad_frames: bfloat16 [8, 512, 1024], P(('rep', 'dp'), 'ctx')
- grad_out: float32 [512, 1024], P('dp')
Inputs may be any that keep to these rules, and one draw needn't show every extreme that they name: `lengths`: number of real frames of each meeting; one meeting of every draw has all 512 frames real.
All inputs are finite; a program needn't handle non-finite values.
Results may differ from a plain program's by a relative error of at most 0.025.
The roundings to bfloat16 on the way count: a program that leaves them out, or rounds other values in their place, can miss the bound.
Values may be sent and summed in bfloat16 or wider, within the bound.
A program may use at most 64 MiB of HBM per device.

v0:
```python
import math
import jax
import jax.numpy as jnp
from jax import lax
from jax.sharding import PartitionSpec as P

HEAD = 128
MASKED_SCORE = -1e30


def head_split(matrix, head_count):
    return matrix.reshape(matrix.shape[0], head_count, matrix.shape[1] // head_count)


def forward_step(carry, key_part, value_part, offset, query_heads, length, score_scale):
    head_count = query_heads.shape[1]
    amount = key_part.shape[0]
    maxima, totals, accumulated = carry
    key_heads = head_split(key_part, head_count)
    value_heads = head_split(value_part, head_count)
    scores = (
        jnp.einsum("rhe,nhe->hrn", query_heads, key_heads, preferred_element_type=jnp.float32)
        * score_scale
    )
    usable = offset + jnp.arange(amount) < length
    scores = jnp.where(usable[None, None, :], scores, MASKED_SCORE)
    new_maxima = jnp.maximum(maxima, jnp.max(scores, axis=2))
    factor = jnp.exp(maxima - new_maxima)
    exponent = jnp.where(usable[None, None, :], jnp.exp(scores - new_maxima[:, :, None]), 0.0)
    totals = totals * factor + jnp.sum(exponent, axis=2)
    mixed = jnp.einsum(
        "hrn,nhe->hre",
        exponent.astype(jnp.bfloat16),
        value_heads,
        preferred_element_type=jnp.float32,
    )
    accumulated = accumulated * factor[:, :, None] + mixed
    return (new_maxima, totals, accumulated)


def query_step(
    grad_accum,
    key_part,
    value_part,
    offset,
    query_heads,
    context_heads,
    logsum,
    deltas,
    length,
    score_scale,
):
    head_count = query_heads.shape[1]
    amount = key_part.shape[0]
    key_heads = head_split(key_part, head_count)
    value_heads = head_split(value_part, head_count)
    scores = (
        jnp.einsum("rhe,nhe->hrn", query_heads, key_heads, preferred_element_type=jnp.float32)
        * score_scale
    )
    usable = offset + jnp.arange(amount) < length
    attention = jnp.where(usable[None, None, :], jnp.exp(scores - logsum[:, :, None]), 0.0)
    grad_prob = jnp.einsum(
        "rhe,nhe->hrn", context_heads, value_heads, preferred_element_type=jnp.float32
    )
    grad_score = (attention * (grad_prob - deltas[:, :, None])).astype(jnp.bfloat16)
    added = jnp.einsum("hrn,nhe->rhe", grad_score, key_heads, preferred_element_type=jnp.float32)
    return grad_accum + added * score_scale


def key_step(
    query_part,
    context_part,
    all_logsum,
    all_deltas,
    key_heads,
    value_heads,
    key_usable,
    score_scale,
):
    head_count = key_heads.shape[1]
    query_heads = head_split(query_part, head_count)
    context_heads = head_split(context_part, head_count)
    scores = (
        jnp.einsum("rhe,nhe->hrn", query_heads, key_heads, preferred_element_type=jnp.float32)
        * score_scale
    )
    attention = jnp.where(key_usable[None, None, :], jnp.exp(scores - all_logsum[:, :, None]), 0.0)
    grad_value = jnp.einsum(
        "hrn,rhe->nhe",
        attention.astype(jnp.bfloat16),
        context_heads,
        preferred_element_type=jnp.float32,
    )
    grad_prob = jnp.einsum(
        "rhe,nhe->hrn", context_heads, value_heads, preferred_element_type=jnp.float32
    )
    grad_score = (attention * (grad_prob - all_deltas[:, :, None])).astype(jnp.bfloat16)
    added = jnp.einsum("hrn,rhe->nhe", grad_score, query_heads, preferred_element_type=jnp.float32)
    return (added * score_scale, grad_value)


def back_project(gradient, weight):
    return lax.dot_general(
        gradient, weight, (((1,), (1,)), ((), ())), preferred_element_type=jnp.float32
    )


def shards(frames, lengths, cotangent, w_query, w_key, w_value, w_out):
    full_query, full_key, full_value, full_out = (
        lax.all_gather(w_query, "dp", axis=0, tiled=True),
        lax.all_gather(w_key, "dp", axis=0, tiled=True),
        lax.all_gather(w_value, "dp", axis=0, tiled=True),
        lax.all_gather(w_out, "dp", axis=0, tiled=True),
    )
    inputs = frames[0]
    upstream = cotangent[0]
    length = lengths[0]
    row_count = inputs.shape[0]
    inner_width = full_query.shape[1]
    head_count = inner_width // HEAD
    score_scale = HEAD ** (-0.5)
    first_frame = lax.axis_index("ctx") * row_count
    row_usable = first_frame + jnp.arange(row_count) < length
    queries = jnp.dot(inputs, full_query, preferred_element_type=jnp.float32).astype(jnp.bfloat16)
    keys = jnp.dot(inputs, full_key, preferred_element_type=jnp.float32).astype(jnp.bfloat16)
    values = jnp.dot(inputs, full_value, preferred_element_type=jnp.float32).astype(jnp.bfloat16)
    query_heads = head_split(queries, head_count)
    key_heads = head_split(keys, head_count)
    value_heads = head_split(values, head_count)
    start_state = (
        jnp.full((head_count, row_count), MASKED_SCORE, jnp.float32),
        jnp.zeros((head_count, row_count), jnp.float32),
        jnp.zeros((head_count, row_count, HEAD), jnp.float32),
    )
    all_keys, all_values = (
        lax.all_gather(keys, "ctx", axis=0, tiled=True),
        lax.all_gather(values, "ctx", axis=0, tiled=True),
    )
    key_block = row_count * math.gcd(max(1, 512 // row_count), lax.axis_size("ctx"))
    block_count = all_keys.shape[0] // key_block
    key_blocks = all_keys.reshape(block_count, key_block, inner_width)
    value_blocks = all_values.reshape(block_count, key_block, inner_width)
    block_starts = jnp.arange(block_count, dtype=jnp.int32) * key_block

    def scan_forward(current, scan_item):
        return (
            forward_step(
                current, scan_item[0], scan_item[1], scan_item[2], query_heads, length, score_scale
            ),
            None,
        )

    softmax_state, unused = lax.scan(
        scan_forward, start_state, (key_blocks, value_blocks, block_starts)
    )
    maxima, totals, accumulated = softmax_state
    context = (
        (accumulated / totals[:, :, None])
        .transpose(1, 0, 2)
        .reshape(row_count, inner_width)
        .astype(jnp.bfloat16)
    )
    logsum = maxima + jnp.log(totals)
    attended = jnp.dot(context, full_out, preferred_element_type=jnp.float32)
    attended = jnp.where(row_usable[:, None], attended, 0.0).astype(jnp.bfloat16)
    masked_grad = jnp.where(row_usable[:, None], upstream, jnp.zeros_like(upstream))
    grad_context = back_project(masked_grad, full_out).astype(jnp.bfloat16)
    deltas = jnp.sum(
        (grad_context.astype(jnp.float32) * context.astype(jnp.float32)).reshape(
            row_count, head_count, HEAD
        ),
        axis=2,
    )
    context_heads = head_split(grad_context, head_count)
    delta_heads = deltas.T
    all_logsum, all_deltas = (
        lax.all_gather(logsum, "ctx", axis=1, tiled=True),
        lax.all_gather(delta_heads, "ctx", axis=1, tiled=True),
    )
    zero_grad = jnp.zeros((row_count, head_count, HEAD), jnp.float32)

    def scan_query(current, scan_item):
        return (
            query_step(
                current,
                scan_item[0],
                scan_item[1],
                scan_item[2],
                query_heads,
                context_heads,
                logsum,
                delta_heads,
                length,
                score_scale,
            ),
            None,
        )

    grad_query, unused = lax.scan(scan_query, zero_grad, (key_blocks, value_blocks, block_starts))
    grad_key, grad_value = key_step(
        lax.all_gather(queries, "ctx", axis=0, tiled=True),
        lax.all_gather(grad_context, "ctx", axis=0, tiled=True),
        all_logsum,
        all_deltas,
        key_heads,
        value_heads,
        row_usable,
        score_scale,
    )
    grad_query = grad_query.reshape(row_count, inner_width).astype(jnp.bfloat16)
    grad_key = grad_key.reshape(row_count, inner_width).astype(jnp.bfloat16)
    grad_value = grad_value.reshape(row_count, inner_width).astype(jnp.bfloat16)
    grad_input = (
        back_project(grad_query, full_query)
        + back_project(grad_key, full_key)
        + back_project(grad_value, full_value)
    )
    grad_frames = grad_input.astype(jnp.bfloat16)
    summed_grad = lax.psum(
        lax.dot_general(
            context, masked_grad, (((0,), (0,)), ((), ())), preferred_element_type=jnp.float32
        ),
        ("rep", "ctx"),
    )
    grad_out = lax.psum_scatter(summed_grad, "dp", scatter_dimension=0, tiled=True)
    return (attended[None], grad_frames[None], grad_out)


def solution(mesh):
    in_specs = (
        P(("rep", "dp"), "ctx", None),
        P(("rep", "dp")),
        P(("rep", "dp"), "ctx", None),
        P("dp", None),
        P("dp", None),
        P("dp", None),
        P("dp", None),
    )
    out_specs = (P(("rep", "dp"), "ctx", None), P(("rep", "dp"), "ctx", None), P("dp", None))
    return jax.shard_map(shards, mesh=mesh, in_specs=in_specs, out_specs=out_specs, check_vma=False)
```

profile of v0, /device:TPU:0, one launch (start us, length us, event | category | flops | bytes accessed | tf_op | source)
XLA Modules:
  0.0 236.2 jit_solution(8206433220303085801)
XLA Ops:
  7.2 0.0 copy-start
  7.2 0.0 all-gather.9.cloned.1.call-start
  7.2 0.7 all-gather.9.cloned.1.call-update
  7.9 0.0 all-gather.7.cloned.1.call-start
  8.0 0.7 all-gather.7.cloned.1.call-update
  8.7 0.0 all-gather.5.cloned.1.call-start
  8.7 0.7 all-gather.5.cloned.1.call-update
  9.4 0.0 all-gather.11.cloned.1.call-start
  9.4 0.5 all-gather.11.cloned.1.call-update
  10.0 0.0 reduce-scatter.2.cloned.1.call-start
  10.7 0.0 copy-start.10
  10.7 18.3 %all-gather.9.cloned.1.call-done = bf16[1024,512]{1,0:T(8,128)(2,1)} async-done(((bf16[256,512]{1,0:T(8,128)(2,1)}), bf16[1024,512]{1,0:T(8,128)(2,1)}) %all-gather.9.cloned.1.call-update) | async-done | bytes 1048592 | tf_op jit(solution)/shard_map/all_gather | solution.py:113
  29.0 0.0 copy-done
  29.0 1.5 convolution_convert_fusion.2
  30.6 16.1 %all_gather.34 = bf16[512,512]{1,0:T(8,128)(2,1)S(1)} all-gather(bf16[128,512]{1,0:T(8,128)(2,1)S(1)} %convolution_convert_fusion.2), channel_id=1, replica_groups=mesh['rep'=2,'dp'=4,'ctx'=4] {'ctx'}, dimensions={0}, use_global_device_ids=true | all-gather | bytes 655360 | tf_op jit(solution)/shard_map/all_gather | solution.py:138
  46.6 0.2 copy.33
  46.9 0.0 copy-start.6
  46.9 0.5 all-gather.7.cloned.1.call-done
  47.4 1.5 convolution_convert_fusion.3
  48.9 0.0 copy-start.7
  48.9 16.0 %all_gather.32 = bf16[512,512]{1,0:T(8,128)(2,1)S(1)} all-gather(bf16[128,512]{1,0:T(8,128)(2,1)S(1)} %convolution_convert_fusion.3), channel_id=1, replica_groups=mesh['rep'=2,'dp'=4,'ctx'=4] {'ctx'}, dimensions={0}, use_global_device_ids=true | all-gather | bytes 655360 | tf_op jit(solution)/shard_map/all_gather | solution.py:137
  64.9 0.2 copy.35
  65.1 0.5 all-gather.5.cloned.1.call-done
  65.7 1.5 convolution_convert_fusion.4
  67.2 0.0 copy-done.7
  67.2 0.4 select_reduce_fusion
  67.6 0.0 copy-start.5
  67.6 0.3 fusion.23
  68.0 0.0 copy-done.10
  68.0 0.0 copy-done.6
  68.0 0.4 fusion.19
  68.4 0.2 copy-done.5
  68.6 1.8 fusion.36
  70.4 0.0 reduce-scatter.2.cloned.1.call-update
  70.4 0.0 all-reduce.2.cloned.1.call-start
  70.5 0.1 copy.22
  70.6 0.8 copy.34
  71.3 12.5 %all-gather.11.cloned.1.call-done = bf16[512,1024]{1,0:T(8,128)(2,1)} async-done(((bf16[128,1024]{1,0:T(8,128)(2,1)}), bf16[512,1024]{1,0:T(8,128)(2,1)}) %all-gather.11.cloned.1.call-update) | async-done | bytes 1048592 | tf_op jit(solution)/shard_map/all_gather | solution.py:114
  83.9 1.7 convert_multiply_fusion
  85.6 0.0 copy-start.8
  85.6 0.1 reshape.104
  85.7 0.2 reduce_sum.23
  85.9 0.6 copy.23
  86.5 16.1 %all_gather.36 = bf16[512,512]{1,0:T(8,128)(2,1)S(1)} all-gather(bf16[128,512]{1,0:T(8,128)(2,1)S(1)} %convolution_convert_fusion.4), channel_id=1, replica_groups=mesh['rep'=2,'dp'=4,'ctx'=4] {'ctx'}, dimensions={0}, use_global_device_ids=true | all-gather | bytes 655360 | tf_op jit(solution)/shard_map/all_gather | solution.py:202
  102.6 1.1 copy.36
  103.6 16.0 %all_gather.38 = bf16[512,512]{1,0:T(8,128)(2,1)S(1)} all-gather(bf16[128,512]{1,0:T(8,128)(2,1)S(1)} %get-tuple-element.50), channel_id=1, replica_groups=mesh['rep'=2,'dp'=4,'ctx'=4] {'ctx'}, dimensions={0}, use_global_device_ids=true | all-gather | bytes 655360 | tf_op jit(solution)/shard_map/all_gather | solution.py:203
  119.6 0.2 copy.37
  119.8 0.0 copy-done.8
  119.8 14.3 %all_gather.39 = f32[4,512]{0,1:T(8,128)S(1)} all-gather(f32[4,128]{0,1:T(8,128)S(1)} %bitcast.109), channel_id=1, replica_groups=mesh['rep'=2,'dp'=4,'ctx'=4] {'ctx'}, dimensions={1}, use_global_device_ids=true | all-gather | bytes 10240 | tf_op jit(solution)/shard_map/all_gather | solution.py:179
  134.1 0.1 copy.27
  134.2 11.9 %all_gather.37 = f32[4,512]{1,0:T(4,128)S(1)} all-gather(f32[4,128]{1,0:T(4,128)S(1)} %get-tuple-element.36), channel_id=1, replica_groups=mesh['rep'=2,'dp'=4,'ctx'=4] {'ctx'}, dimensions={1}, use_global_device_ids=true | all-gather | bytes 10240 | tf_op jit(solution)/shard_map/all_gather | solution.py:178
  146.1 1.6 fusion.3
  147.6 1.0 convolution_convert_fusion
  148.7 2.3 fusion.18
  151.0 0.0 copy-done.4
  151.0 2.7 %fusion.60 = f32[128,1024]{1,0:T(8,128)} fusion(bf16[128,512]{0,1:T(8,128)(2,1)} %bitcast.115, bf16[1024,512]{1,0:T(8,128)(2,1)} %all-gather.5.cloned.1.call-done), kind=kOutput, calls=%fused_computation.80 | convolution fusion | flops 134217728 | bytes 1703936 | tf_op jit(solution)/shard_map/dot_general | solution.py:104
  153.7 2.9 %fusion.17 = bf16[4,128,128]{2,1,0:T(8,128)(2,1)} fusion(bf16[512,4,128]{0,2,1:T(8,128)(2,1)} %bitcast.104, f32[4,512,128]{2,1,0:T(8,128)} %copy-done.4, bf16[512,4,128]{0,2,1:T(8,128)(2,1)S(1)} %bitcast.100, bf16[128,4,128]{0,2,1:T(8,128)(2,1)} %bitcast.111, f32[4,512]{1,0:T(4,128)S(1)} %copy.27), kind=kOutput, calls=%fused_computation.30 | convolution fusion | flops 135135232 | bytes 2367488 | tf_op jit(solution)/shard_map/hrn,rhe->nhe/dot_general | solution.py:99
  156.6 0.0 all-reduce.2.cloned.1.call-update
  156.6 1.0 fusion.14
  157.6 0.0 copy-done.1
  157.6 1.6 convolution_add_fusion.1
  159.3 1.2 fusion.13
  160.4 67.1 %all-reduce.2.cloned.1.call-done = f32[128,1024]{1,0:T(8,128)} async-done(((f32[128,1024]{1,0:T(8,128)}), f32[128,1024]{1,0:T(8,128)}) %all-reduce.2.cloned.1.call-update) | async-done | bytes 524304 | tf_op jit(solution)/shard_map/psum | solution.py:220
  227.5 1.9 copy.58
  (14 shorter events, 0.1 us)
Async XLA Ops:
  7.2 21.9 %copy-start = (bf16[1,128,1024]{2,1,0:T(8,128)(2,1)S(1)}, bf16[1,128,1024]{2,1,0:T(8,128)(2,1)}, u32[]{:S(2)}) copy-start(bf16[1,128,1024]{2,1,0:T(8,128)(2,1)} %param.7) | copy-start | bytes 786436
  7.2 21.9 %all-gather.9.cloned.1.call-start = ((), (), s32[]{:S(2)}) async-start(), calls=%async_computation.3 | async-start | bytes 1310720 | tf_op jit(solution)/shard_map/all_gather | solution.py:113
  7.9 39.4 %all-gather.7.cloned.1.call-start = ((), (), s32[]{:S(2)}) async-start(), calls=%async_computation.2 | async-start | bytes 1310720 | tf_op jit(solution)/shard_map/all_gather | solution.py:112
  8.7 57.0 %all-gather.5.cloned.1.call-start = ((), (), s32[]{:S(2)}) async-start(), calls=%async_computation.1 | async-start | bytes 1310720 | tf_op jit(solution)/shard_map/all_gather | solution.py:111
  9.4 74.5 %all-gather.11.cloned.1.call-start = ((), (), s32[]{:S(2)}) async-start(), calls=%async_computation.4 | async-start | bytes 1310720 | tf_op jit(solution)/shard_map/all_gather | solution.py:114
  10.0 146.6 %reduce-scatter.2.cloned.1.call-start = ((), (), s32[]{:S(2)}) async-start(), calls=%async_computation.5 | async-start | bytes 2621440 | tf_op jit(solution)/shard_map/reduce_scatter | solution.py:226
  10.7 57.3 %copy-start.10 = (pred[512]{0:T(512)(128)(4,1)}, pred[512]{0:T(512)(128)(4,1)S(1)}, u32[]{:S(2)}) copy-start(pred[512]{0:T(512)(128)(4,1)S(1)} %iota_compare_fusion) | copy-start | bytes 1540
  46.9 21.1 %copy-start.6 = (bf16[512,512]{0,1:T(8,128)(2,1)}, bf16[512,512]{0,1:T(8,128)(2,1)S(1)}, u32[]{:S(2)}) copy-start(bf16[512,512]{0,1:T(8,128)(2,1)S(1)} %copy.33) | copy-start | bytes 1572868
  48.9 18.3 %copy-start.7 = (bf16[128,512]{1,0:T(8,128)(2,1)}, bf16[128,512]{1,0:T(8,128)(2,1)S(1)}, u32[]{:S(2)}) copy-start(bf16[128,512]{1,0:T(8,128)(2,1)S(1)} %convolution_convert_fusion.3) | copy-start | bytes 393220
  67.6 1.0 copy-start.5
  70.4 157.1 %all-reduce.2.cloned.1.call-start = ((), (), s32[]{:S(2)}) async-start(), calls=%async_computation.6 | async-start | bytes 1048576 | tf_op jit(solution)/shard_map/psum | solution.py:220
  85.6 34.3 %copy-start.8 = (bf16[128,512]{1,0:T(8,128)(2,1)}, bf16[128,512]{1,0:T(8,128)(2,1)S(1)}, u32[]{:S(2)}) copy-start(bf16[128,512]{1,0:T(8,128)(2,1)S(1)} %get-tuple-element.50) | copy-start | bytes 393220
  147.6 3.4 %copy-start.4 = (f32[4,512,128]{2,1,0:T(8,128)}, f32[4,512,128]{2,1,0:T(8,128)S(1)}, u32[]{:S(2)}) copy-start(f32[4,512,128]{2,1,0:T(8,128)S(1)} %fusion.3) | copy-start | bytes 3145732
  151.0 5.6 %copy-start.2 = (bf16[512,1024]{1,0:T(8,128)(2,1)S(1)}, bf16[512,1024]{1,0:T(8,128)(2,1)}, u32[]{:S(2)}) copy-start(bf16[512,1024]{1,0:T(8,128)(2,1)} %all-gather.11.cloned.1.call-done) | copy-start | bytes 3145732
  153.7 4.0 %copy-start.1 = (bf16[1024,512]{1,0:T(8,128)(2,1)S(1)}, bf16[1024,512]{1,0:T(8,128)(2,1)}, u32[]{:S(2)}) copy-start(bf16[1024,512]{1,0:T(8,128)(2,1)} %all-gather.7.cloned.1.call-done) | copy-start | bytes 3145732
  156.6 2.7 %copy-start.3 = (bf16[1024,512]{1,0:T(8,128)(2,1)S(1)}, bf16[1024,512]{1,0:T(8,128)(2,1)}, u32[]{:S(2)}) copy-start(bf16[1024,512]{1,0:T(8,128)(2,1)} %all-gather.9.cloned.1.call-done) | copy-start | bytes 3145732
  156.6 2.7 %copy-start.9 = (bf16[4,128,128]{2,1,0:T(8,128)(2,1)S(1)}, bf16[4,128,128]{2,1,0:T(8,128)(2,1)}, u32[]{:S(2)}) copy-start(bf16[4,128,128]{2,1,0:T(8,128)(2,1)} %convolution_convert_fusion) | copy-start | bytes 393220
Sparse Core Ops, SparseCore 0:
  9.6 19.4 all-gather.8
  30.6 16.7 all-gather.6
  48.9 16.7 all-gather.4
  67.1 16.7 all-gather.10
  86.2 31.4 reduce-scatter.1
  156.7 70.7 all-reduce.1
where the time goes:
time: 237 us; the launch traced here: 236 us
  waiting for transfers between devices  102 us (43%)
  blocking collectives  90.2 us (38%)
  matrix products  23.2 us (10%)
  between operations  15 us (6%)
  local copies, waits for them, and re-layouts  5.47 us (2%)
    psum x1, waiting for transfers between devices, shards(): lax.psum(lax.dot_general(context, masked_grad, (((0,), (0,)), ((), ())),...  67.1 us
    all_gather x1, waiting for transfers between devices, shards(): lax.all_gather(w_value, 'dp', axis=0, tiled=True)  18.3 us
    all_gather x1, blocking collectives, shards(): lax.all_gather(values, 'ctx', axis=0, tiled=True)  16.1 us
    all_gather x1, blocking collectives, shards(): lax.all_gather(queries, 'ctx', axis=0, tiled=True)  16.1 us
    all_gather x1, blocking collectives, shards(): lax.all_gather(keys, 'ctx', axis=0, tiled=True)  16 us
    all_gather x1, blocking collectives, shards(): lax.all_gather(grad_context, 'ctx', axis=0, tiled=True)  16 us
    all_gather x1, blocking collectives, shards(): lax.all_gather(delta_heads, 'ctx', axis=1, tiled=True)  14.3 us
    all_gather x1, waiting for transfers between devices, shards(): lax.all_gather(w_out, 'dp', axis=0, tiled=True)  12.5 us
  transfers between devices with their start and end apart: 6, of which 5 were waited for; matrix products, arithmetic and copies ran while one was open for 11% of the time, Pallas kernels for 0%

commit v1 on v0

--- a/solution.py
+++ b/solution.py
@@ -217,11 +217,14 @@
         + back_project(grad_value, full_value)
     )
     grad_frames = grad_input.astype(jnp.bfloat16)
-    summed_grad = lax.psum(
-        lax.dot_general(
-            context, masked_grad, (((0,), (0,)), ((), ())), preferred_element_type=jnp.float32
+    summed_grad = jnp.sum(
+        lax.all_gather(
+            lax.dot_general(
+                context, masked_grad, (((0,), (0,)), ((), ())), preferred_element_type=jnp.float32
+            ),
+            ("rep", "ctx"),
         ),
-        ("rep", "ctx"),
+        axis=0,
     )
     grad_out = lax.psum_scatter(summed_grad, "dp", scatter_dimension=0, tiled=True)
     return (attended[None], grad_frames[None], grad_out)

time: 237 us -> 411 us (1.73)
  waiting for transfers between devices: 102 us -> 266 us
  other arithmetic: 0.59 us -> 9.94 us
    all_gather x0 -> x1, waiting for transfers between devices: none -> 228 us  [shards(): lax.all_gather(lax.dot_general(context, masked_grad, (((0,), (0,)), ((),...]
    psum x1 -> x0, waiting for transfers between devices: 67.1 us -> none  [shards(): lax.psum(lax.dot_general(context, masked_grad, (((0,), (0,)), ((), ())),...]
    all_gather x1, waiting for transfers between devices: 0.49 us -> 18.9 us  [shards(): lax.all_gather(w_key, 'dp', axis=0, tiled=True)]
    all_gather x1, waiting for transfers between devices: 12.5 us -> 0.01 us  [shards(): lax.all_gather(w_out, 'dp', axis=0, tiled=True)]
    reduce_sum x0 -> x1, other arithmetic: none -> 9.35 us  [shards(): jnp.sum(lax.all_gather(lax.dot_general(context, masked_grad, (((0,), (0,)...]
  transfers between devices with their start and end apart: 6 -> 6, of which waited for: 5 -> 4; matrix products, arithmetic and copies ran while one was open for 11% -> 8% of each run, Pallas kernels for 0% -> 0%
where the time goes in v1:
time: 411 us; the launch traced here: 410 us
  waiting for transfers between devices  266 us (65%)
  blocking collectives  90.3 us (22%)
  matrix products  22 us (5%)
  between operations  15 us (4%)
  other arithmetic  9.94 us (2%)
  local copies, waits for them, and re-layouts  7.28 us (2%)
    all_gather x1, waiting for transfers between devices, shards(): lax.all_gather(lax.dot_general(context, masked_grad, (((0,), (0,)), ((),...  228 us
    all_gather x1, waiting for transfers between devices, shards(): lax.all_gather(w_key, 'dp', axis=0, tiled=True)  18.9 us
    all_gather x1, blocking collectives, shards(): lax.all_gather(grad_context, 'ctx', axis=0, tiled=True)  16.7 us
    all_gather x1, blocking collectives, shards(): lax.all_gather(values, 'ctx', axis=0, tiled=True)  16.1 us
    all_gather x1, blocking collectives, shards(): lax.all_gather(keys, 'ctx', axis=0, tiled=True)  16.1 us
    all_gather x1, waiting for transfers between devices, shards(): lax.all_gather(w_value, 'dp', axis=0, tiled=True)  16 us
    all_gather x1, blocking collectives, shards(): lax.all_gather(queries, 'ctx', axis=0, tiled=True)  15.4 us
    all_gather x1, blocking collectives, shards(): lax.all_gather(delta_heads, 'ctx', axis=1, tiled=True)  14.2 us
  transfers between devices with their start and end apart: 6, of which 4 were waited for; matrix products, arithmetic and copies ran while one was open for 8% of the time, Pallas kernels for 0%

profile of v1, /device:TPU:0, one launch (start us, length us, event | category | flops | bytes accessed | tf_op | source)
XLA Modules:
  0.0 410.2 jit_solution(10125585143240210003)
XLA Ops:
  7.2 0.0 copy-start
  7.2 0.0 all-gather.9.cloned.1.call-start
  7.2 0.7 all-gather.9.cloned.1.call-update
  7.9 0.0 all-gather.7.cloned.1.call-start
  8.0 0.7 all-gather.7.cloned.1.call-update
  8.7 0.0 all-gather.11.cloned.1.call-start
  8.7 0.7 all-gather.11.cloned.1.call-update
  9.4 0.0 all-gather.15.cloned.1.call-start
  10.1 0.0 copy-start.10
  10.1 18.9 %all-gather.9.cloned.1.call-done = bf16[1024,512]{1,0:T(8,128)(2,1)} async-done(((bf16[256,512]{1,0:T(8,128)(2,1)}), bf16[1024,512]{1,0:T(8,128)(2,1)}) %all-gather.9.cloned.1.call-update) | async-done | bytes 1048592 | tf_op jit(solution)/shard_map/all_gather | solution.py:112
  29.0 0.0 copy-done
  29.0 1.5 convolution_convert_fusion.3
  30.6 0.0 copy-start.7
  30.6 16.1 %all_gather.38 = bf16[512,512]{1,0:T(8,128)(2,1)S(1)} all-gather(bf16[128,512]{1,0:T(8,128)(2,1)S(1)} %convolution_convert_fusion.3), channel_id=1, replica_groups=mesh['rep'=2,'dp'=4,'ctx'=4] {'ctx'}, dimensions={0}, use_global_device_ids=true | all-gather | bytes 655360 | tf_op jit(solution)/shard_map/all_gather | solution.py:137
  46.6 0.2 copy.35
  46.9 0.5 all-gather.7.cloned.1.call-done
  47.3 1.5 convolution_convert_fusion.4
  48.9 0.0 copy-done.7
  48.9 0.4 select_reduce_fusion
  49.3 0.3 fusion.23
  49.7 16.0 %all-gather.11.cloned.1.call-done = bf16[1024,512]{1,0:T(8,128)(2,1)} async-done(((bf16[256,512]{1,0:T(8,128)(2,1)}), bf16[1024,512]{1,0:T(8,128)(2,1)}) %all-gather.11.cloned.1.call-update) | async-done | bytes 1048592 | tf_op jit(solution)/shard_map/all_gather | solution.py:113
  65.7 1.5 convolution_convert_fusion.2
  67.2 16.1 %all_gather.40 = bf16[512,512]{1,0:T(8,128)(2,1)S(1)} all-gather(bf16[128,512]{1,0:T(8,128)(2,1)S(1)} %convolution_convert_fusion.2), channel_id=1, replica_groups=mesh['rep'=2,'dp'=4,'ctx'=4] {'ctx'}, dimensions={0}, use_global_device_ids=true | all-gather | bytes 655360 | tf_op jit(solution)/shard_map/all_gather | solution.py:138
  83.3 1.0 copy.33
  84.3 0.0 copy-done.10
  84.3 1.4 fusion.19
  85.7 0.0 copy-done.6
  85.7 1.8 fusion.36
  87.6 0.0 all-gather.15.cloned.1.call-update
  87.6 0.0 all-gather.13.cloned.1.call-start
  87.7 0.5 all-gather.13.cloned.1.call-update
  88.2 0.0 reduce-scatter.2.cloned.1.call-start
  88.2 227.5 %all-gather.15.cloned.1.call-done = f32[4096,1024]{1,0:T(8,128)} async-done(((f32[512,1024]{1,0:T(8,128)}), f32[4096,1024]{1,0:T(8,128)}) %all-gather.15.cloned.1.call-update) | async-done | bytes 16777232 | tf_op jit(solution)/shard_map/all_gather | solution.py:221
  315.8 9.3 %reduce_sum.33 = f32[512,1024]{1,0:T(8,128)} reduce(f32[8,512,1024]{2,1,0:T(8,128)} %bitcast.100, f32[]{:T(128)} %constant.28.clone.1), dimensions={0}, to_apply=%region_3.4 | reduce | flops 3670016 | bytes 18874372 | tf_op jit(solution)/shard_map/reduce_sum | solution.py:220
  325.1 0.0 reduce-scatter.2.cloned.1.call-update
  325.1 0.8 copy.34
  325.9 0.8 copy.22
  326.7 15.4 %all_gather.42 = bf16[512,512]{1,0:T(8,128)(2,1)S(1)} all-gather(bf16[128,512]{1,0:T(8,128)(2,1)S(1)} %convolution_convert_fusion.4), channel_id=1, replica_groups=mesh['rep'=2,'dp'=4,'ctx'=4] {'ctx'}, dimensions={0}, use_global_device_ids=true | all-gather | bytes 655360 | tf_op jit(solution)/shard_map/all_gather | solution.py:202
  342.1 1.0 copy.36
  343.1 2.5 convert_multiply_fusion
  345.6 0.1 reshape.104
  345.7 0.2 reduce_sum.32
  345.9 0.7 copy.23
  346.6 14.2 %all_gather.45 = f32[4,512]{0,1:T(8,128)S(1)} all-gather(f32[4,128]{0,1:T(8,128)S(1)} %bitcast.111), channel_id=1, replica_groups=mesh['rep'=2,'dp'=4,'ctx'=4] {'ctx'}, dimensions={1}, use_global_device_ids=true | all-gather | bytes 10240 | tf_op jit(solution)/shard_map/all_gather | solution.py:179
  360.8 0.1 copy.27
  360.9 16.7 %all_gather.44 = bf16[512,512]{1,0:T(8,128)(2,1)} all-gather(bf16[128,512]{1,0:T(8,128)(2,1)} %get-tuple-element.50), channel_id=1, replica_groups=mesh['rep'=2,'dp'=4,'ctx'=4] {'ctx'}, dimensions={0}, use_global_device_ids=true | all-gather | bytes 655360 | tf_op jit(solution)/shard_map/all_gather | solution.py:203
  377.6 1.3 copy.37
  378.8 11.9 %all_gather.43 = f32[4,512]{1,0:T(4,128)S(1)} all-gather(f32[4,128]{1,0:T(4,128)S(1)} %get-tuple-element.36), channel_id=1, replica_groups=mesh['rep'=2,'dp'=4,'ctx'=4] {'ctx'}, dimensions={1}, use_global_device_ids=true | all-gather | bytes 10240 | tf_op jit(solution)/shard_map/all_gather | solution.py:178
  390.7 0.0 copy-done.2
  390.7 1.0 fusion.14
  391.7 1.6 fusion.3
  393.3 1.0 copy-done.5
  394.3 1.0 convolution_convert_fusion
  395.3 0.0 copy-done.8
  395.3 2.3 fusion.18
  397.6 1.5 fusion.60
  399.1 0.0 copy-start.3
  399.1 2.2 fusion.17
  401.3 0.0 copy-start.9
  401.3 0.0 copy-done.1
  401.3 0.5 convolution_add_fusion.1
  401.8 0.0 copy-done.3
  401.8 0.4 copy-done.9
  402.2 1.2 fusion.13
  (14 shorter events, 0.1 us)
Async XLA Ops:
  7.2 21.9 %copy-start = (bf16[1,128,1024]{2,1,0:T(8,128)(2,1)S(1)}, bf16[1,128,1024]{2,1,0:T(8,128)(2,1)}, u32[]{:S(2)}) copy-start(bf16[1,128,1024]{2,1,0:T(8,128)(2,1)} %param.7) | copy-start | bytes 786436
  7.2 21.9 %all-gather.9.cloned.1.call-start = ((), (), s32[]{:S(2)}) async-start(), calls=%async_computation.2 | async-start | bytes 1310720 | tf_op jit(solution)/shard_map/all_gather | solution.py:112
  7.9 39.4 %all-gather.7.cloned.1.call-start = ((), (), s32[]{:S(2)}) async-start(), calls=%async_computation.1 | async-start | bytes 1310720 | tf_op jit(solution)/shard_map/all_gather | solution.py:111
  8.7 57.0 %all-gather.11.cloned.1.call-start = ((), (), s32[]{:S(2)}) async-start(), calls=%async_computation.3 | async-start | bytes 1310720 | tf_op jit(solution)/shard_map/all_gather | solution.py:113
  9.4 306.4 %all-gather.15.cloned.1.call-start = ((), (), s32[]{:S(2)}) async-start(), calls=%async_computation.6 | async-start | bytes 18874368 | tf_op jit(solution)/shard_map/all_gather | solution.py:221
  10.1 74.2 %copy-start.10 = (pred[512]{0:T(512)(128)(4,1)}, pred[512]{0:T(512)(128)(4,1)S(1)}, u32[]{:S(2)}) copy-start(pred[512]{0:T(512)(128)(4,1)S(1)} %iota_compare_fusion) | copy-start | bytes 1540
  30.6 18.3 %copy-start.7 = (bf16[128,512]{1,0:T(8,128)(2,1)}, bf16[128,512]{1,0:T(8,128)(2,1)S(1)}, u32[]{:S(2)}) copy-start(bf16[128,512]{1,0:T(8,128)(2,1)S(1)} %convolution_convert_fusion.3) | copy-start | bytes 393220
  83.3 2.5 copy-start.6
  87.6 255.5 %all-gather.13.cloned.1.call-start = ((), (), s32[]{:S(2)}) async-start(), calls=%async_computation.4 | async-start | bytes 1310720 | tf_op jit(solution)/shard_map/all_gather | solution.py:114
  88.2 315.2 %reduce-scatter.2.cloned.1.call-start = ((), (), s32[]{:S(2)}) async-start(), calls=%async_computation.5 | async-start | bytes 2621440 | tf_op jit(solution)/shard_map/reduce_scatter | solution.py:229
  343.1 47.6 %copy-start.2 = (bf16[512,1024]{1,0:T(8,128)(2,1)S(1)}, bf16[512,1024]{1,0:T(8,128)(2,1)}, u32[]{:S(2)}) copy-start(bf16[512,1024]{1,0:T(8,128)(2,1)} %all-gather.13.cloned.1.call-done) | copy-start | bytes 3145732
  391.7 3.6 copy-start.8
  393.3 1.0 copy-start.5
  394.3 3.3 copy-start.4
  397.6 3.7 copy-start.1
  399.1 2.8 copy-start.3
  401.3 0.9 copy-start.9
Sparse Core Ops, SparseCore 0:
  9.6 19.4 all-gather.8
  30.6 16.7 all-gather.6
  48.9 16.7 all-gather.10
  87.7 227.9 all-gather.14
  317.2 14.9 all-gather.12
  335.1 31.4 reduce-scatter.1
